TPU v7x, 256 devices: a whole 4x4x8 slice. The times are simulated.
256 devices in a mesh: dp: 16 (over x, y), expert: 16 (over z, core).
Axes of the slice: x: 4, y: 4, z: 8, core: 2. Of those that a mesh axis runs over, the one named last changes fastest.
Arguments:
- tokens: bfloat16 [40960, 2048], P(('dp', 'expert')), may hold values from -6 to 6
- routes: int32 [40960, 2], P(('dp', 'expert')), may hold values from 0 to 15, all different within a row; in each aligned block of 160 rows (0 to 159, 160 to 319, ...) at most 30 rows name the same one
- route_gains: float32 [40960, 2], P(('dp', 'expert')), may hold values from 0.1 to 1
- cotangent: bfloat16 [40960, 2048], P(('dp', 'expert')), may hold values from -24 to 24
- w_gate: bfloat16 [16, 2048, 768], P('expert'), may hold values from -0.125 to 0.125
- w_up: bfloat16 [16, 2048, 768], P('expert'), may hold values from -0.125 to 0.125
- w_down: bfloat16 [16, 2048, 768], P('expert'), may hold values from -0.21875 to 0.21875
Outputs:
- layer_output: bfloat16 [40960, 2048], P(('dp', 'expert'))
- input_grad: bfloat16 [40960, 2048], P(('dp', 'expert'))
- grad_gate: bfloat16 [16, 2048, 768], P('expert', 'dp')
- grad_up: bfloat16 [16, 2048, 768], P('expert', 'dp')
- grad_down: bfloat16 [16, 2048, 768], P('expert', 'dp')
Inputs may be any that keep to these rules, and one draw needn't show every extreme that they name: `routes`: each row names 2 different experts. Within the rows of one device (aligned blocks of 160 rows) no expert is named more than 30 times, and in some device's rows one expert is named exactly 30 times.
All inputs are finite; a program needn't handle non-finite values.
Results may differ from a plain program's by a relative error of at most 0.015.
Values may be sent and summed in bfloat16 or wider, within the bound.
A program may use at most 128 MiB of HBM per device.

v0:
```python
import jax
import jax.numpy as jnp
from jax import lax
from jax.sharding import PartitionSpec as P

SLOTS = 32


def slot_masks(routes, experts):
    rows, picks = routes.shape
    chosen = routes.T.reshape(1, -1)
    labels = lax.broadcasted_iota(jnp.int32, (experts, rows * picks), 0)
    matches = chosen == labels
    total = rows * picks
    earlier = lax.broadcasted_iota(jnp.int32, (total, total), 0) < lax.broadcasted_iota(
        jnp.int32, (total, total), 1
    )
    before = jnp.dot(
        matches.astype(jnp.bfloat16),
        earlier.astype(jnp.bfloat16),
        preferred_element_type=jnp.float32,
    )
    position = jnp.sum(jnp.where(matches, before, 0.0), axis=0).astype(jnp.int32)
    target = chosen[0] * SLOTS + position
    slots = lax.broadcasted_iota(jnp.int32, (experts * SLOTS, total), 0)
    return (slots == target[None, :]).reshape(experts * SLOTS, picks, rows)


def rows_t(left, right):
    return lax.dot_general(
        left, right, (((1,), (1,)), ((), ())), preferred_element_type=jnp.float32
    )


def outer_rows(left, right):
    return lax.dot_general(
        left, right, (((0,), (0,)), ((), ())), preferred_element_type=jnp.float32
    )


def shards(tokens, routes, route_gains, cotangent, w_gate, w_up, w_down):
    experts = lax.axis_size("expert")
    groups = lax.axis_size("dp")
    width = tokens.shape[1]
    depth = width // groups
    flip = [(a * experts + b, b * experts + a) for a in range(groups) for b in range(experts)]
    mine = lax.axis_index("dp") * depth
    hidden_units = w_gate.shape[2]

    def fetch(w):
        part = lax.dynamic_slice_in_dim(w[0], mine, depth, axis=0)
        return part

    part = jnp.concatenate([fetch(w_gate), fetch(w_up), fetch(w_down)], axis=1)
    part = lax.ppermute(part, ("dp", "expert"), flip)
    full = lax.all_gather(part, "expert", axis=0, tiled=True)
    gate_mat = full[:, :hidden_units]
    up_mat = full[:, hidden_units : 2 * hidden_units]
    down_mat = full[:, 2 * hidden_units :]
    masks = slot_masks(routes, groups)
    first = masks[:, 0, :].astype(jnp.bfloat16)
    second = masks[:, 1, :].astype(jnp.bfloat16)
    both = first + second
    gains = route_gains.T
    slot_gain = jnp.sum(jnp.where(masks, gains[None], 0.0), axis=(1, 2))
    send_tok = jnp.dot(both, tokens, preferred_element_type=jnp.float32).astype(jnp.bfloat16)
    send_cot = (
        slot_gain[:, None] * jnp.dot(both, cotangent, preferred_element_type=jnp.float32)
    ).astype(jnp.bfloat16)

    def exchange(block):
        block = block.reshape(groups, SLOTS, width)
        block = lax.all_to_all(block, "dp", split_axis=0, concat_axis=0, tiled=True)
        return block.reshape(groups * SLOTS, width)

    arrived = exchange(send_tok)
    arrived_cot = exchange(send_cot)
    pre_gate = jnp.dot(arrived, gate_mat, preferred_element_type=jnp.float32)
    pre_up = jnp.dot(arrived, up_mat, preferred_element_type=jnp.float32)
    sigma = jax.nn.sigmoid(pre_gate)
    activated = pre_gate * sigma
    hidden = (activated * pre_up).astype(jnp.bfloat16)
    d_hidden = jnp.dot(arrived_cot, down_mat, preferred_element_type=jnp.float32)
    d_gate = (d_hidden * pre_up * (sigma * (1.0 + pre_gate * (1.0 - sigma)))).astype(jnp.bfloat16)
    d_up = (d_hidden * activated).astype(jnp.bfloat16)
    partial = jnp.concatenate(
        [outer_rows(arrived, d_gate), outer_rows(arrived, d_up), outer_rows(arrived_cot, hidden)],
        axis=1,
    ).astype(jnp.bfloat16)
    summed = lax.psum_scatter(partial, "expert", scatter_dimension=0, tiled=True)
    produced = rows_t(hidden, down_mat).astype(jnp.bfloat16)
    d_pick = (rows_t(d_gate, gate_mat) + rows_t(d_up, up_mat)).astype(jnp.bfloat16)
    back_out = exchange(produced)
    back_grad = exchange(d_pick)
    layer_output = (
        gains[0][:, None] * outer_rows(first, back_out)
        + gains[1][:, None] * outer_rows(second, back_out)
    ).astype(jnp.bfloat16)
    input_grad = (outer_rows(first, back_grad) + outer_rows(second, back_grad)).astype(jnp.bfloat16)
    summed = lax.ppermute(summed, ("dp", "expert"), flip)
    grad_gate = summed[None, :, :hidden_units]
    grad_up = summed[None, :, hidden_units : 2 * hidden_units]
    grad_down = summed[None, :, 2 * hidden_units :]
    return (layer_output, input_grad, grad_gate, grad_up, grad_down)


def solution(mesh):
    rows = P(("dp", "expert"), None)
    weights = P("expert", None, None)
    shares = P("expert", "dp", None)
    return jax.shard_map(
        shards,
        mesh=mesh,
        in_specs=(rows, rows, rows, rows, weights, weights, weights),
        out_specs=(rows, rows, shares, shares, shares),
        check_vma=False,
    )
```

profile of v0, /device:TPU:14, one launch (start us, length us, event | category | flops | bytes accessed | tf_op | source)
XLA Modules:
  0.0 330.9 jit_solution(815282746643636325)
XLA Ops:
  10.3 7.4 %collective-permute-start = (bf16[128,2304]{1,0:T(8,128)(2,1)S(1)}, bf16[128,2304]{1,0:T(8,128)(2,1)S(1)}, u32[]{:S(2)}, u32[]{:S(2)}) collective-permute-start(bf16[128,2304]{1,0:T(8,128)(2,1)S(1)} %pad_maximum_fusion.1), channel_id=1, source_target_pairs={{0,0},{1,16},{2,32},{3,48},{4,64},{5,80},{6,96},{7,112},{8,128},{9... | collective-permute-start | bytes 1769480 | tf_op jit(solution)/shard_map/ppermute | solution.py:55
  17.7 56.6 %collective-permute-done = bf16[128,2304]{1,0:T(8,128)(2,1)S(1)} collective-permute-done((bf16[128,2304]{1,0:T(8,128)(2,1)S(1)}, bf16[128,2304]{1,0:T(8,128)(2,1)S(1)}, u32[]{:S(2)}, u32[]{:S(2)}) %collective-permute-start) | collective-permute-done | bytes 589856 | tf_op jit(solution)/shard_map/ppermute | solution.py:55
  78.1 5.6 %all-to-all-start.2 = ((bf16[16,32,2048]{2,1,0:T(8,128)(2,1)}), bf16[16,32,2048]{2,1,0:T(8,128)(2,1)S(1)}, u32[]{:S(2)}, u32[]{:S(2)}) async-start(bf16[16,32,2048]{2,1,0:T(8,128)(2,1)} %bitcast.72), calls=%async_computation.2 | async-start | bytes 4194304 | tf_op jit(solution)/shard_map/all_to_all | solution.py:73
  85.8 23.9 %all-to-all-done.2 = bf16[16,32,2048]{2,1,0:T(8,128)(2,1)S(1)} async-done(((bf16[16,32,2048]{2,1,0:T(8,128)(2,1)}), bf16[16,32,2048]{2,1,0:T(8,128)(2,1)S(1)}, u32[]{:S(2)}, u32[]{:S(2)}) %all-to-all-start.2) | async-done | bytes 2097184 | tf_op jit(solution)/shard_map/all_to_all | solution.py:73
  109.6 7.3 %all-to-all-start = ((bf16[16,32,2048]{2,1,0:T(8,128)(2,1)}), bf16[16,32,2048]{2,1,0:T(8,128)(2,1)}, u32[]{:S(2)}, u32[]{:S(2)}) async-start(bf16[16,32,2048]{2,1,0:T(8,128)(2,1)} %bitcast.5), calls=%async_computation | async-start | bytes 4194304 | tf_op jit(solution)/shard_map/all_to_all | solution.py:73
  117.2 18.1 %all-gather.2.cloned.1.call-done = bf16[2048,2304]{1,0:T(8,128)(2,1)} async-done(((bf16[128,2304]{1,0:T(8,128)(2,1)}), bf16[2048,2304]{1,0:T(8,128)(2,1)}) %all-gather.2.cloned.1.call-update) | async-done | bytes 9437200 | tf_op jit(solution)/shard_map/all_gather | solution.py:56
  135.3 4.8 %fusion = f32[512,768]{1,0:T(8,128)} fusion(bf16[512,2048]{1,0:T(8,128)(2,1)S(1)} %bitcast.68, bf16[2048,2304]{1,0:T(8,128)(2,1)} %all-gather.2.cloned.1.call-done), kind=kOutput, calls=%fused_computation.8 | convolution fusion | flops 1610612736 | bytes 6815744 | tf_op jit(solution)/shard_map/dot_general | solution.py:83
  140.2 4.4 %fusion.5 = f32[512,768]{1,0:T(8,128)S(1)} fusion(bf16[512,2048]{1,0:T(8,128)(2,1)} %bitcast.6, bf16[2048,2304]{1,0:T(8,128)(2,1)} %all-gather.2.cloned.1.call-done), kind=kOutput, calls=%fused_computation.13 | convolution fusion | flops 1610612736 | bytes 6815744 | tf_op jit(solution)/shard_map/dot_general | solution.py:79
  144.7 5.0 %multiply_convert_fusion.2 = (bf16[512,768]{1,0:T(8,128)(2,1)S(1)}, bf16[512,768]{1,0:T(8,128)(2,1)S(1)}, bf16[512,768]{1,0:T(8,128)(2,1)S(1)}) fusion(f32[512,768]{1,0:T(8,128)S(1)} %copy-done.16, f32[512,768]{1,0:T(8,128)S(1)} %fusion.5, bf16[512,2048]{1,0:T(8,128)(2,1)} %bitcast.6, bf16[2048,2304]{1,0:T(8,128)(2,1)} %all-gather.2.cloned.1.call-done), kind=kOutput, calls=%fused_computation.25 | convolution fusion | flops 1616510976 | bytes 10747904 | tf_op jit(solution)/shard_map/dot_general | solution.py:78
  151.6 3.4 %convolution_convert_fusion.1 = bf16[2048,768]{0,1:T(8,128)(2,1)S(1)} fusion(bf16[512,2048]{1,0:T(8,128)(2,1)} %bitcast.6, bf16[512,768]{1,0:T(8,128)(2,1)S(1)} %get-tuple-element.26), kind=kOutput, calls=%fused_computation.4 | convolution fusion | flops 1612185600 | bytes 6029312 | tf_op jit(solution)/shard_map/dot_general | solution.py:36
  155.0 3.4 %convolution_convert_fusion.2 = bf16[2048,768]{0,1:T(8,128)(2,1)S(1)} fusion(bf16[512,2048]{1,0:T(8,128)(2,1)} %bitcast.6, bf16[512,768]{1,0:T(8,128)(2,1)S(1)} %get-tuple-element.25), kind=kOutput, calls=%fused_computation.5 | convolution fusion | flops 1612185600 | bytes 6029312 | tf_op jit(solution)/shard_map/dot_general | solution.py:36
  158.5 4.7 %pad_maximum_fusion = bf16[2048,2304]{0,1:T(8,128)(2,1)} fusion(bf16[2048,768]{0,1:T(8,128)(2,1)S(1)} %convolution_convert_fusion, bf16[2048,768]{0,1:T(8,128)(2,1)S(1)} %convolution_convert_fusion.1, bf16[2048,768]{0,1:T(8,128)(2,1)S(1)} %convolution_convert_fusion.2), kind=kLoop, calls=%fused_computation | loop fusion | flops 28311552 | bytes 18874368 | tf_op jit(solution)/shard_map/concatenate | solution.py:86
  163.1 12.4 %copy.25 = bf16[2048,2304]{1,0:T(8,128)(2,1)} copy(bf16[2048,2304]{0,1:T(8,128)(2,1)} %pad_maximum_fusion) | data formatting | bytes 18874368
  176.6 3.8 %fusion.3 = f32[512,2048]{1,0:T(8,128)S(1)} fusion(bf16[512,768]{1,0:T(8,128)(2,1)S(1)} %copy-done.15, bf16[2048,2304]{1,0:T(8,128)(2,1)} %all-gather.2.cloned.1.call-done), kind=kOutput, calls=%fused_computation.11 | convolution fusion | flops 1610612736 | bytes 8126464 | tf_op jit(solution)/shard_map/dot_general | solution.py:30
  180.4 5.1 %add_convert_fusion = bf16[512,2048]{1,0:T(8,128)(2,1)} fusion(f32[512,2048]{1,0:T(8,128)S(1)} %fusion.3, bf16[512,768]{1,0:T(8,128)(2,1)S(1)} %copy-done.13, bf16[2048,2304]{1,0:T(8,128)(2,1)} %all-gather.2.cloned.1.call-done), kind=kOutput, calls=%fused_computation.1 | convolution fusion | flops 1612709888 | bytes 10223616 | tf_op jit(solution)/shard_map/dot_general | solution.py:30
  185.5 8.2 %all-to-all-start.3 = ((bf16[16,32,2048]{2,1,0:T(8,128)(2,1)}), bf16[16,32,2048]{2,1,0:T(8,128)(2,1)S(1)}, u32[]{:S(2)}, u32[]{:S(2)}) async-start(bf16[16,32,2048]{2,1,0:T(8,128)(2,1)} %bitcast.71), calls=%async_computation.3 | async-start | bytes 4194304 | tf_op jit(solution)/shard_map/all_to_all | solution.py:73
  193.8 5.0 %convolution_convert_fusion.4 = bf16[512,2048]{1,0:T(8,128)(2,1)} fusion(bf16[512,768]{1,0:T(8,128)(2,1)S(1)} %copy-done.18, bf16[2048,2304]{1,0:T(8,128)(2,1)} %all-gather.2.cloned.1.call-done), kind=kOutput, calls=%fused_computation.7 | convolution fusion | flops 1611661312 | bytes 6029312 | tf_op jit(solution)/shard_map/dot_general | solution.py:30
  198.8 21.2 %all-to-all-done.3 = bf16[16,32,2048]{2,1,0:T(8,128)(2,1)S(1)} async-done(((bf16[16,32,2048]{2,1,0:T(8,128)(2,1)}), bf16[16,32,2048]{2,1,0:T(8,128)(2,1)S(1)}, u32[]{:S(2)}, u32[]{:S(2)}) %all-to-all-start.3) | async-done | bytes 2097184 | tf_op jit(solution)/shard_map/all_to_all | solution.py:73
  221.3 7.0 %all-to-all-start.1 = ((bf16[16,32,2048]{2,1,0:T(8,128)(2,1)}), bf16[16,32,2048]{2,1,0:T(8,128)(2,1)S(1)}, u32[]{:S(2)}, u32[]{:S(2)}) async-start(bf16[16,32,2048]{2,1,0:T(8,128)(2,1)} %bitcast.70), calls=%async_computation.1 | async-start | bytes 4194304 | tf_op jit(solution)/shard_map/all_to_all | solution.py:73
  228.4 2.3 fusion.15
  232.1 20.1 %reduce-scatter.4.cloned.1.call-done = bf16[128,2304]{1,0:T(8,128)(2,1)} async-done(((bf16[2048,2304]{1,0:T(8,128)(2,1)}), bf16[128,2304]{1,0:T(8,128)(2,1)}) %reduce-scatter.4.cloned.1.call-update) | async-done | bytes 589840
  252.2 2.1 copy.26
  258.2 3.2 fusion.12
  261.3 57.5 %collective-permute-done.1 = bf16[128,2304]{0,1:T(8,128)(2,1)} collective-permute-done((bf16[128,2304]{0,1:T(8,128)(2,1)}, bf16[128,2304]{0,1:T(8,128)(2,1)}, u32[]{:S(2)}, u32[]{:S(2)}) %collective-permute-start.1) | collective-permute-done | bytes 589856 | tf_op jit(solution)/shard_map/ppermute | solution.py:100
  (67 shorter events, 23.9 us)
Async XLA Ops:
  7.2 1.9 copy-start
  7.2 68.0 %copy-start.10 = (f32[160,2]{0,1:T(2,128)S(1)}, f32[160,2]{0,1:T(2,128)}, u32[]{:S(2)}) copy-start(f32[160,2]{0,1:T(2,128)} %param.9) | copy-start | bytes 3844
  7.2 68.1 %copy-start.9 = (s32[160,2]{0,1:T(2,128)S(1)}, s32[160,2]{0,1:T(2,128)}, u32[]{:S(2)}) copy-start(s32[160,2]{0,1:T(2,128)} %param.8) | copy-start | bytes 3844
  7.2 128.1 %all-gather.2.cloned.1.call-start = ((), (), s32[]{:S(2)}) async-start(), calls=%async_computation.5 | async-start | bytes 10027008 | tf_op jit(solution)/shard_map/all_gather | solution.py:56
  9.1 66.9 %copy-start.11 = (bf16[160,2048]{1,0:T(8,128)(2,1)S(1)}, bf16[160,2048]{1,0:T(8,128)(2,1)}, u32[]{:S(2)}) copy-start(bf16[160,2048]{1,0:T(8,128)(2,1)} %param.10) | copy-start | bytes 1966084
  10.3 64.1 %collective-permute-start = (bf16[128,2304]{1,0:T(8,128)(2,1)S(1)}, bf16[128,2304]{1,0:T(8,128)(2,1)S(1)}, u32[]{:S(2)}, u32[]{:S(2)}) collective-permute-start(bf16[128,2304]{1,0:T(8,128)(2,1)S(1)} %pad_maximum_fusion.1), channel_id=1, source_target_pairs={{0,0},{1,16},{2,32},{3,48},{4,64},{5,80},{6,96},{7,112},{8,128},{9... | collective-permute-start | bytes 1769480 | tf_op jit(solution)/shard_map/ppermute | solution.py:55
  78.1 5.6 %copy-start.7 = (bf16[160,2048]{1,0:T(8,128)(2,1)S(1)}, bf16[160,2048]{1,0:T(8,128)(2,1)}, u32[]{:S(2)}) copy-start(bf16[160,2048]{1,0:T(8,128)(2,1)} %param.7) | copy-start | bytes 1966084
  78.1 31.5 %all-to-all-start.2 = ((bf16[16,32,2048]{2,1,0:T(8,128)(2,1)}), bf16[16,32,2048]{2,1,0:T(8,128)(2,1)S(1)}, u32[]{:S(2)}, u32[]{:S(2)}) async-start(bf16[16,32,2048]{2,1,0:T(8,128)(2,1)} %bitcast.72), calls=%async_computation.2 | async-start | bytes 4194304 | tf_op jit(solution)/shard_map/all_to_all | solution.py:73
  109.6 25.7 %copy-start.5 = (bf16[16,32,2048]{2,1,0:T(8,128)(2,1)}, bf16[16,32,2048]{2,1,0:T(8,128)(2,1)S(1)}, u32[]{:S(2)}) copy-start(bf16[16,32,2048]{2,1,0:T(8,128)(2,1)S(1)} %all-to-all-done.2) | copy-start | bytes 6291460
  109.6 30.6 %all-to-all-start = ((bf16[16,32,2048]{2,1,0:T(8,128)(2,1)}), bf16[16,32,2048]{2,1,0:T(8,128)(2,1)}, u32[]{:S(2)}, u32[]{:S(2)}) async-start(bf16[16,32,2048]{2,1,0:T(8,128)(2,1)} %bitcast.5), calls=%async_computation | async-start | bytes 4194304 | tf_op jit(solution)/shard_map/all_to_all | solution.py:73
  117.0 135.2 %reduce-scatter.4.cloned.1.call-start = ((), (), s32[]{:S(2)}) async-start(), calls=%async_computation.6 | async-start | bytes 10027008
  140.2 4.4 %copy-start.16 = (f32[512,768]{1,0:T(8,128)S(1)}, f32[512,768]{1,0:T(8,128)}, u32[]{:S(2)}) copy-start(f32[512,768]{1,0:T(8,128)} %fusion) | copy-start | bytes 4718596
  144.7 5.0 %copy-start.6 = (bf16[16,32,2048]{2,1,0:T(8,128)(2,1)S(1)}, bf16[16,32,2048]{2,1,0:T(8,128)(2,1)}, u32[]{:S(2)}) copy-start(bf16[16,32,2048]{2,1,0:T(8,128)(2,1)} %copy-done.5) | copy-start | bytes 6291460
  149.7 1.9 copy-start.17
  149.7 1.9 copy-start.14
  149.7 5.3 %copy-start.12 = (bf16[512,768]{1,0:T(8,128)(2,1)}, bf16[512,768]{1,0:T(8,128)(2,1)S(1)}, u32[]{:S(2)}) copy-start(bf16[512,768]{1,0:T(8,128)(2,1)S(1)} %get-tuple-element.25) | copy-start | bytes 2359300
  176.6 3.8 %copy-start.13 = (bf16[512,768]{1,0:T(8,128)(2,1)S(1)}, bf16[512,768]{1,0:T(8,128)(2,1)}, u32[]{:S(2)}) copy-start(bf16[512,768]{1,0:T(8,128)(2,1)} %copy-done.12) | copy-start | bytes 2359300
  185.5 8.3 %copy-start.18 = (bf16[512,768]{1,0:T(8,128)(2,1)S(1)}, bf16[512,768]{1,0:T(8,128)(2,1)}, u32[]{:S(2)}) copy-start(bf16[512,768]{1,0:T(8,128)(2,1)} %copy-done.17) | copy-start | bytes 2359300
  185.5 34.5 %all-to-all-start.3 = ((bf16[16,32,2048]{2,1,0:T(8,128)(2,1)}), bf16[16,32,2048]{2,1,0:T(8,128)(2,1)S(1)}, u32[]{:S(2)}, u32[]{:S(2)}) async-start(bf16[16,32,2048]{2,1,0:T(8,128)(2,1)} %bitcast.71), calls=%async_computation.3 | async-start | bytes 4194304 | tf_op jit(solution)/shard_map/all_to_all | solution.py:73
  221.3 34.9 %all-to-all-start.1 = ((bf16[16,32,2048]{2,1,0:T(8,128)(2,1)}), bf16[16,32,2048]{2,1,0:T(8,128)(2,1)S(1)}, u32[]{:S(2)}, u32[]{:S(2)}) async-start(bf16[16,32,2048]{2,1,0:T(8,128)(2,1)} %bitcast.70), calls=%async_computation.1 | async-start | bytes 4194304 | tf_op jit(solution)/shard_map/all_to_all | solution.py:73
  228.4 2.4 copy-start.4
  254.4 64.5 %collective-permute-start.1 = (bf16[128,2304]{0,1:T(8,128)(2,1)}, bf16[128,2304]{0,1:T(8,128)(2,1)}, u32[]{:S(2)}, u32[]{:S(2)}) collective-permute-start(bf16[128,2304]{0,1:T(8,128)(2,1)} %copy.26), channel_id=1, source_target_pairs={{0,0},{1,16},{2,32},{3,48},{4,64},{5,80},{6,96},{7,112},{8,128},{9... | collective-permute-start | bytes 1769480 | tf_op jit(solution)/shard_map/ppermute | solution.py:100
  256.3 1.4 copy-start.2
  258.2 65.9 %copy-start.1 = (bf16[1,2048,768]{2,1,0:T(8,128)(2,1)S(1)}, bf16[1,2048,768]{2,1,0:T(8,128)(2,1)}, u32[]{:S(2)}) copy-start(bf16[1,2048,768]{2,1,0:T(8,128)(2,1)} %param.11) | copy-start | bytes 9437188
  (3 other events, 3.3 us)
Sparse Core Ops, SparseCore 0:
  75.3 59.9 all-gather.1
  175.6 76.5 reduce-scatter.3
where the time goes:
time: 332 us; the launch traced here: 331 us
  waiting for transfers between devices  198 us (60%)
  matrix products  48.6 us (15%)
  starting transfers between devices  37.8 us (11%)
  local copies, waits for them, and re-layouts  27.6 us (8%)
  between operations  14.3 us (4%)
  other arithmetic  5.04 us (2%)
    ppermute x1, waiting for transfers between devices, shards(): summed = lax.ppermute(summed, ('dp', 'expert'), flip)  57.5 us
    ppermute x1, waiting for transfers between devices, shards(): part = lax.ppermute(part, ('dp', 'expert'), flip)  56.6 us
    all_to_all x4, waiting for transfers between devices, exchange(): block = lax.all_to_all(block, 'dp', split_axis=0, concat_axis=0, tiled=True)  45.1 us
    all_to_all x4, starting transfers between devices, exchange(): block = lax.all_to_all(block, 'dp', split_axis=0, concat_axis=0, tiled=True)  28.2 us
    unnamed x43, local copies, waits for them, and re-layouts  24.4 us
    unnamed x3, waiting for transfers between devices  20.2 us
    all_gather x1, waiting for transfers between devices, shards(): full = lax.all_gather(part, 'expert', axis=0, tiled=True)  18.1 us
    dot_general x7, matrix products, outer_rows(): lax.dot_general(left, right, (((0,), (0,)), ((), ())), preferred_element_...  16.1 us
  transfers between devices with their start and end apart: 8, of which 7 were waited for; matrix products, arithmetic and copies ran while one was open for 10% of the time, Pallas kernels for 0%

commit v1 on v0

--- a/solution.py
+++ b/solution.py
@@ -53,7 +53,9 @@
 
     part = jnp.concatenate([fetch(w_gate), fetch(w_up), fetch(w_down)], axis=1)
     part = lax.ppermute(part, ("dp", "expert"), flip)
-    full = lax.all_gather(part, "expert", axis=0, tiled=True)
+    full = jnp.concatenate(
+        lax.all_to_all(jnp.stack([part] * lax.axis_size("expert")), "expert", 0, 0), axis=0
+    )
     gate_mat = full[:, :hidden_units]
     up_mat = full[:, hidden_units : 2 * hidden_units]
     down_mat = full[:, 2 * hidden_units :]

time: 332 us -> 536 us (1.61)
  waiting for transfers between devices: 198 us -> 378 us
  starting transfers between devices: 37.8 us -> 56.4 us
    all_to_all x0 -> x1, waiting for transfers between devices: none -> 205 us  [shards(): lax.all_to_all(jnp.stack([part] * lax.axis_size('expert')), 'expert', 0, 0)]
    all_to_all x0 -> x1, starting transfers between devices: none -> 18.8 us  [shards(): lax.all_to_all(jnp.stack([part] * lax.axis_size('expert')), 'expert', 0, 0)]
    all_gather x1 -> x0, waiting for transfers between devices: 18.1 us -> none  [shards(): full = lax.all_gather(part, 'expert', axis=0, tiled=True)]
    unnamed x43 -> x37, local copies, waits for them, and re-layouts: 24.4 us -> 22 us
    unnamed x3 -> x2, waiting for transfers between devices: 20.2 us -> 18.8 us
  transfers between devices with their start and end apart: 8 -> 8, of which waited for: 7 -> 6; matrix products, arithmetic and copies ran while one was open for 10% -> 6% of each run, Pallas kernels for 0% -> 0%
where the time goes in v1:
time: 536 us; the launch traced here: 535 us
  waiting for transfers between devices  378 us (71%)
  starting transfers between devices  56.4 us (11%)
  matrix products  49.3 us (9%)
  local copies, waits for them, and re-layouts  31.2 us (6%)
  between operations  14.3 us (3%)
  other arithmetic  5.73 us (1%)
    all_to_all x1, waiting for transfers between devices, shards(): lax.all_to_all(jnp.stack([part] * lax.axis_size('expert')), 'expert', 0, 0)  205 us
    ppermute x1, waiting for transfers between devices, shards(): summed = lax.ppermute(summed, ('dp', 'expert'), flip)  57.5 us
    ppermute x1, waiting for transfers between devices, shards(): part = lax.ppermute(part, ('dp', 'expert'), flip)  57.2 us
    all_to_all x4, waiting for transfers between devices, exchange(): block = lax.all_to_all(block, 'dp', split_axis=0, concat_axis=0, tiled=True)  39.8 us
    all_to_all x4, starting transfers between devices, exchange(): block = lax.all_to_all(block, 'dp', split_axis=0, concat_axis=0, tiled=True)  28.5 us
    unnamed x37, local copies, waits for them, and re-layouts  22 us
    unnamed x2, waiting for transfers between devices  18.8 us
    all_to_all x1, starting transfers between devices, shards(): lax.all_to_all(jnp.stack([part] * lax.axis_size('expert')), 'expert', 0, 0)  18.8 us
  transfers between devices with their start and end apart: 8, of which 6 were waited for; matrix products, arithmetic and copies ran while one was open for 6% of the time, Pallas kernels for 0%

profile of v1, /device:TPU:14, one launch (start us, length us, event | category | flops | bytes accessed | tf_op | source)
XLA Modules:
  0.0 534.8 jit_solution(11185797284566019626)
XLA Ops:
  10.2 3.2 multiply_convert_fusion
  13.4 7.3 %all-to-all-start.3 = ((bf16[16,32,2048]{2,1,0:T(8,128)(2,1)}), bf16[16,32,2048]{2,1,0:T(8,128)(2,1)}, u32[]{:S(2)}, u32[]{:S(2)}) async-start(bf16[16,32,2048]{2,1,0:T(8,128)(2,1)} %bitcast.69), calls=%async_computation.3 | async-start | bytes 4194304 | tf_op jit(solution)/shard_map/all_to_all | solution.py:75
  21.9 7.0 %collective-permute-start = (bf16[128,2304]{1,0:T(8,128)(2,1)S(1)}, bf16[128,2304]{1,0:T(8,128)(2,1)S(1)}, u32[]{:S(2)}, u32[]{:S(2)}) collective-permute-start(bf16[128,2304]{1,0:T(8,128)(2,1)S(1)} %pad_maximum_fusion.1), channel_id=1, source_target_pairs={{0,0},{1,16},{2,32},{3,48},{4,64},{5,80},{6,96},{7,112},{8,128},{9... | collective-permute-start | bytes 1769480 | tf_op jit(solution)/shard_map/ppermute | solution.py:55
  28.8 57.2 %collective-permute-done = bf16[128,2304]{1,0:T(8,128)(2,1)S(1)} collective-permute-done((bf16[128,2304]{1,0:T(8,128)(2,1)S(1)}, bf16[128,2304]{1,0:T(8,128)(2,1)S(1)}, u32[]{:S(2)}, u32[]{:S(2)}) %collective-permute-start) | collective-permute-done | bytes 589856 | tf_op jit(solution)/shard_map/ppermute | solution.py:55
  86.1 4.5 stack.2
  90.6 18.8 %all-to-all-start.1 = ((bf16[16,128,2304]{2,1,0:T(8,128)(2,1)}), bf16[16,128,2304]{2,1,0:T(8,128)(2,1)}, u32[]{:S(2)}, u32[]{:S(2)}) async-start(bf16[16,128,2304]{2,1,0:T(8,128)(2,1)} %stack.2), calls=%async_computation.1 | async-start | bytes 18874368 | tf_op jit(solution)/shard_map/all_to_all | solution.py:57
  111.5 204.5 %all-to-all-done.1 = bf16[16,128,2304]{2,1,0:T(8,128)(2,1)} async-done(((bf16[16,128,2304]{2,1,0:T(8,128)(2,1)}), bf16[16,128,2304]{2,1,0:T(8,128)(2,1)}, u32[]{:S(2)}, u32[]{:S(2)}) %all-to-all-start.1) | async-done | bytes 9437216 | tf_op jit(solution)/shard_map/all_to_all | solution.py:57
  316.0 5.9 %all-to-all-start = ((bf16[16,32,2048]{2,1,0:T(8,128)(2,1)}), bf16[16,32,2048]{2,1,0:T(8,128)(2,1)S(1)}, u32[]{:S(2)}, u32[]{:S(2)}) async-start(bf16[16,32,2048]{2,1,0:T(8,128)(2,1)} %bitcast.5), calls=%async_computation | async-start | bytes 4194304 | tf_op jit(solution)/shard_map/all_to_all | solution.py:75
  322.1 5.6 %fusion = f32[512,768]{1,0:T(8,128)} fusion(bf16[512,2048]{1,0:T(8,128)(2,1)} %bitcast.15, bf16[2048,2304]{1,0:T(8,128)(2,1)} %bitcast.10), kind=kOutput, calls=%fused_computation.8 | convolution fusion | flops 1610612736 | bytes 6815744 | tf_op jit(solution)/shard_map/dot_general | solution.py:85
  327.7 20.7 %all-to-all-done = bf16[16,32,2048]{2,1,0:T(8,128)(2,1)S(1)} async-done(((bf16[16,32,2048]{2,1,0:T(8,128)(2,1)}), bf16[16,32,2048]{2,1,0:T(8,128)(2,1)S(1)}, u32[]{:S(2)}, u32[]{:S(2)}) %all-to-all-start) | async-done | bytes 2097184 | tf_op jit(solution)/shard_map/all_to_all | solution.py:75
  348.5 4.5 fusion.5
  353.0 4.3 multiply_convert_fusion.2
  357.3 4.3 convolution_convert_fusion
  365.4 4.7 pad_maximum_fusion
  370.1 12.7 %copy.25 = bf16[2048,2304]{1,0:T(8,128)(2,1)} copy(bf16[2048,2304]{0,1:T(8,128)(2,1)} %pad_maximum_fusion) | data formatting | bytes 18874368
  383.9 3.8 fusion.3
  387.7 5.1 add_convert_fusion
  392.8 7.4 %all-to-all-start.4 = ((bf16[16,32,2048]{2,1,0:T(8,128)(2,1)}), bf16[16,32,2048]{2,1,0:T(8,128)(2,1)S(1)}, u32[]{:S(2)}, u32[]{:S(2)}) async-start(bf16[16,32,2048]{2,1,0:T(8,128)(2,1)} %bitcast.75), calls=%async_computation.4 | async-start | bytes 4194304 | tf_op jit(solution)/shard_map/all_to_all | solution.py:75
  400.1 5.1 convolution_convert_fusion.4
  405.2 19.1 %all-to-all-done.4 = bf16[16,32,2048]{2,1,0:T(8,128)(2,1)S(1)} async-done(((bf16[16,32,2048]{2,1,0:T(8,128)(2,1)}), bf16[16,32,2048]{2,1,0:T(8,128)(2,1)S(1)}, u32[]{:S(2)}, u32[]{:S(2)}) %all-to-all-start.4) | async-done | bytes 2097184 | tf_op jit(solution)/shard_map/all_to_all | solution.py:75
  425.7 7.9 %all-to-all-start.2 = ((bf16[16,32,2048]{2,1,0:T(8,128)(2,1)}), bf16[16,32,2048]{2,1,0:T(8,128)(2,1)S(1)}, u32[]{:S(2)}, u32[]{:S(2)}) async-start(bf16[16,32,2048]{2,1,0:T(8,128)(2,1)} %bitcast.70), calls=%async_computation.2 | async-start | bytes 4194304 | tf_op jit(solution)/shard_map/all_to_all | solution.py:75
  437.3 18.8 %reduce-scatter.4.cloned.1.call-done = bf16[128,2304]{1,0:T(8,128)(2,1)} async-done(((bf16[2048,2304]{1,0:T(8,128)(2,1)}), bf16[128,2304]{1,0:T(8,128)(2,1)}) %reduce-scatter.4.cloned.1.call-update) | async-done | bytes 589840
  462.0 3.2 fusion.12
  465.2 57.5 %collective-permute-done.1 = bf16[128,2304]{0,1:T(8,128)(2,1)} collective-permute-done((bf16[128,2304]{0,1:T(8,128)(2,1)}, bf16[128,2304]{0,1:T(8,128)(2,1)}, u32[]{:S(2)}, u32[]{:S(2)}) %collective-permute-start.1) | collective-permute-done | bytes 589856 | tf_op jit(solution)/shard_map/ppermute | solution.py:102
  (61 shorter events, 27.5 us)
Async XLA Ops:
  7.2 13.5 %copy-start = (bf16[1,2048,768]{2,1,0:T(8,128)(2,1)S(1)}, bf16[1,2048,768]{2,1,0:T(8,128)(2,1)}, u32[]{:S(2)}) copy-start(bf16[1,2048,768]{2,1,0:T(8,128)(2,1)} %param.11) | copy-start | bytes 9437188
  13.4 72.7 %all-to-all-start.3 = ((bf16[16,32,2048]{2,1,0:T(8,128)(2,1)}), bf16[16,32,2048]{2,1,0:T(8,128)(2,1)}, u32[]{:S(2)}, u32[]{:S(2)}) async-start(bf16[16,32,2048]{2,1,0:T(8,128)(2,1)} %bitcast.69), calls=%async_computation.3 | async-start | bytes 4194304 | tf_op jit(solution)/shard_map/all_to_all | solution.py:75
  21.9 64.2 %collective-permute-start = (bf16[128,2304]{1,0:T(8,128)(2,1)S(1)}, bf16[128,2304]{1,0:T(8,128)(2,1)S(1)}, u32[]{:S(2)}, u32[]{:S(2)}) collective-permute-start(bf16[128,2304]{1,0:T(8,128)(2,1)S(1)} %pad_maximum_fusion.1), channel_id=1, source_target_pairs={{0,0},{1,16},{2,32},{3,48},{4,64},{5,80},{6,96},{7,112},{8,128},{9... | collective-permute-start | bytes 1769480 | tf_op jit(solution)/shard_map/ppermute | solution.py:55
  90.6 18.8 %copy-start.7 = (bf16[160,2048]{1,0:T(8,128)(2,1)S(1)}, bf16[160,2048]{1,0:T(8,128)(2,1)}, u32[]{:S(2)}) copy-start(bf16[160,2048]{1,0:T(8,128)(2,1)} %param.7) | copy-start | bytes 1966084
  90.6 225.4 %all-to-all-start.1 = ((bf16[16,128,2304]{2,1,0:T(8,128)(2,1)}), bf16[16,128,2304]{2,1,0:T(8,128)(2,1)}, u32[]{:S(2)}, u32[]{:S(2)}) async-start(bf16[16,128,2304]{2,1,0:T(8,128)(2,1)} %stack.2), calls=%async_computation.1 | async-start | bytes 18874368 | tf_op jit(solution)/shard_map/all_to_all | solution.py:57
  316.0 32.4 %all-to-all-start = ((bf16[16,32,2048]{2,1,0:T(8,128)(2,1)}), bf16[16,32,2048]{2,1,0:T(8,128)(2,1)S(1)}, u32[]{:S(2)}, u32[]{:S(2)}) async-start(bf16[16,32,2048]{2,1,0:T(8,128)(2,1)} %bitcast.5), calls=%async_computation | async-start | bytes 4194304 | tf_op jit(solution)/shard_map/all_to_all | solution.py:75
  321.9 134.2 %reduce-scatter.4.cloned.1.call-start = ((), (), s32[]{:S(2)}) async-start(), calls=%async_computation.6 | async-start | bytes 10027008
  348.5 4.5 copy-start.5
  348.5 4.5 copy-start.13
  357.2 4.4 copy-start.14
  357.2 4.4 copy-start.11
  357.2 6.3 %copy-start.9 = (bf16[512,768]{1,0:T(8,128)(2,1)}, bf16[512,768]{1,0:T(8,128)(2,1)S(1)}, u32[]{:S(2)}) copy-start(bf16[512,768]{1,0:T(8,128)(2,1)S(1)} %get-tuple-element.25) | copy-start | bytes 2359300
  357.3 4.3 copy-start.6
  382.7 1.1 copy-start.12
  383.8 3.8 copy-start.10
  392.8 7.4 %copy-start.15 = (bf16[512,768]{1,0:T(8,128)(2,1)S(1)}, bf16[512,768]{1,0:T(8,128)(2,1)}, u32[]{:S(2)}) copy-start(bf16[512,768]{1,0:T(8,128)(2,1)} %copy-done.14) | copy-start | bytes 2359300
  392.8 31.6 %all-to-all-start.4 = ((bf16[16,32,2048]{2,1,0:T(8,128)(2,1)}), bf16[16,32,2048]{2,1,0:T(8,128)(2,1)S(1)}, u32[]{:S(2)}, u32[]{:S(2)}) async-start(bf16[16,32,2048]{2,1,0:T(8,128)(2,1)} %bitcast.75), calls=%async_computation.4 | async-start | bytes 4194304 | tf_op jit(solution)/shard_map/all_to_all | solution.py:75
  424.3 1.3 copy-start.3
  424.3 9.3 %copy-start.8 = (f32[160,2]{0,1:T(2,128)S(1)}, f32[160,2]{0,1:T(2,128)}, u32[]{:S(2)}) copy-start(f32[160,2]{0,1:T(2,128)} %param.9) | copy-start | bytes 3844
  425.7 34.5 %all-to-all-start.2 = ((bf16[16,32,2048]{2,1,0:T(8,128)(2,1)}), bf16[16,32,2048]{2,1,0:T(8,128)(2,1)S(1)}, u32[]{:S(2)}, u32[]{:S(2)}) async-start(bf16[16,32,2048]{2,1,0:T(8,128)(2,1)} %bitcast.70), calls=%async_computation.2 | async-start | bytes 4194304 | tf_op jit(solution)/shard_map/all_to_all | solution.py:75
  433.6 2.3 copy-start.4
  458.3 64.4 %collective-permute-start.1 = (bf16[128,2304]{0,1:T(8,128)(2,1)}, bf16[128,2304]{0,1:T(8,128)(2,1)}, u32[]{:S(2)}, u32[]{:S(2)}) collective-permute-start(bf16[128,2304]{0,1:T(8,128)(2,1)} %copy.26), channel_id=1, source_target_pairs={{0,0},{1,16},{2,32},{3,48},{4,64},{5,80},{6,96},{7,112},{8,128},{9... | collective-permute-start | bytes 1769480 | tf_op jit(solution)/shard_map/ppermute | solution.py:102
  460.2 1.3 copy-start.2
  462.0 65.9 %copy-start.1 = (bf16[1,2048,768]{2,1,0:T(8,128)(2,1)S(1)}, bf16[1,2048,768]{2,1,0:T(8,128)(2,1)}, u32[]{:S(2)}) copy-start(bf16[1,2048,768]{2,1,0:T(8,128)(2,1)} %param.11) | copy-start | bytes 9437188
Sparse Core Ops, SparseCore 0:
  382.9 73.1 reduce-scatter.3
